TPU v7x, 32 devices: a whole 2x2x4 slice. The times are simulated.
32 devices in a mesh: batch: 8 (over z, core), seq: 4 (over y, x).
Axes of the slice: x: 2, y: 2, z: 4, core: 2. Of those that a mesh axis runs over, the one named last changes fastest.
Arguments:
- hidden_in: bfloat16 [16, 1024, 768], P('batch', 'seq'), may hold values from -7 to 7
- seg_bounds: int32 [16, 65], P('batch'), may hold values from 0 to 1024, as said below
- qkv_weight: bfloat16 [768, 2304], replicated, may hold values from -0.3125 to 0.3125
- query_bias: float32 [768], replicated, may hold values from -3 to 3
- value_bias: float32 [768], replicated, may hold values from -3 to 3
- conv_taps: float32 [12, 33], replicated, may hold values from -3 to 3
- out_weight: bfloat16 [768, 768], replicated, may hold values from -0.21875 to 0.21875
- out_bias: float32 [768], replicated, may hold values from -3 to 3
- first_gain: float32 [768], replicated, may hold values from 0.5 to 1.5
- first_shift: float32 [768], replicated, may hold values from -3 to 3
- up_weight: bfloat16 [768, 3072], replicated, may hold values from -0.21875 to 0.21875
- up_bias: float32 [3072], replicated, may hold values from -3 to 3
- down_weight: bfloat16 [3072, 768], replicated, may hold values from -0.109375 to 0.109375
- down_bias: float32 [768], replicated, may hold values from -3 to 3
- second_gain: float32 [768], replicated, may hold values from 0.5 to 1.5
- second_shift: float32 [768], replicated, may hold values from -3 to 3
- grad_out: bfloat16 [16, 1024, 768], P('batch', 'seq'), may hold values from -6 to 6
Outputs:
- layer_out: bfloat16 [16, 1024, 768], P('batch', 'seq')
- input_grad: bfloat16 [16, 1024, 768], P('batch', 'seq')
- qkv_grad: float32 [768, 2304], replicated
- query_bias_grad: float32 [768], replicated
- value_bias_grad: float32 [768], replicated
- conv_grad: float32 [12, 33], replicated
- out_weight_grad: float32 [768, 768], replicated
- out_bias_grad: float32 [768], replicated
- first_gain_grad: float32 [768], replicated
- first_shift_grad: float32 [768], replicated
- up_weight_grad: float32 [768, 3072], replicated
- up_bias_grad: float32 [3072], replicated
- down_weight_grad: float32 [3072, 768], replicated
- down_bias_grad: float32 [768], replicated
- second_gain_grad: float32 [768], replicated
- second_shift_grad: float32 [768], replicated
- condition: float32 [12], replicated
Inputs may be any that keep to these rules, and one draw needn't show every extreme that they name: `seg_bounds`: each row rises strictly from 0 and ends at the sequence's true length, at least 512; among the 2 sequences of each index of batch one has the length 1024.
All inputs are finite; a program needn't handle non-finite values.
Results may differ from a plain program's by a relative error of at most 0.03.
Values may be sent and summed in bfloat16 or wider, within the bound.
A program may use at most 192 MiB of HBM per device.

v0:
```python
from functools import partial

import jax
import jax.numpy as jnp
from jax import lax
from jax.sharding import PartitionSpec as P

NEWTON = 6


precise = lax.Precision.HIGHEST
epsilon = 1e-05


def with_halo(cells, sides, width):
    for axis, dim in sides:
        count = lax.axis_size(axis)
        ends = count - 1
        head = lax.slice_in_dim(cells, 0, width, axis=dim)
        tail = lax.slice_in_dim(cells, cells.shape[dim] - width, cells.shape[dim], axis=dim)
        cells = jnp.concatenate(
            [
                lax.ppermute(tail, axis, [(i, (i + 1) % count) for i in range(ends)]),
                cells,
                lax.ppermute(head, axis, [((i + 1) % count, i) for i in range(ends)]),
            ],
            axis=dim,
        )
    return cells


def layer_norm(hidden):
    row_mean = jnp.mean(hidden, axis=-1, keepdims=True)
    centered = hidden - row_mean
    inv_std = lax.rsqrt(jnp.mean(centered * centered, axis=-1, keepdims=True) + epsilon)
    return (centered * inv_std, inv_std)


def norm_back(grad_normed, normed, inv_std):
    return inv_std * (
        grad_normed
        - jnp.mean(grad_normed, axis=-1, keepdims=True)
        - normed * jnp.mean(grad_normed * normed, axis=-1, keepdims=True)
    )


def pseudo_inverse(kernel):
    identity = jnp.eye(kernel.shape[-1], dtype=kernel.dtype)
    fro_square = jnp.sum(kernel * kernel, axis=(-2, -1), keepdims=True)
    approx = jnp.swapaxes(kernel, -1, -2) / fro_square
    for newton_step in range(NEWTON):
        product = jnp.matmul(kernel, approx, precision=precise)
        inner_term = 7.0 * identity - product
        inner_term = 15.0 * identity - jnp.matmul(product, inner_term, precision=precise)
        inner_term = 13.0 * identity - jnp.matmul(product, inner_term, precision=precise)
        approx = 0.25 * jnp.matmul(approx, inner_term, precision=precise)
    return approx


def solve_mix(land_query, land_key, kv_mean):
    second_score = jnp.einsum("smhe,snhe->shmn", land_query, land_key, precision=precise)
    kernel_two = jax.nn.softmax(second_score, axis=-1)
    approx = pseudo_inverse(kernel_two)
    mixed_val = jnp.einsum("shmn,shne->shme", approx, kv_mean, precision=precise)
    proxy_vals = jnp.sqrt(jnp.sum(kernel_two * kernel_two, axis=(-2, -1))) * jnp.sqrt(
        jnp.sum(approx * approx, axis=(-2, -1))
    )
    return (mixed_val, proxy_vals)


def heads_split(array, head_count):
    return array.reshape(array.shape[0], array.shape[1], head_count, array.shape[2] // head_count)


def landmark_total(partial_sum, extra_term, counts):
    whole_sum = lax.psum(partial_sum, "seq")
    landmarks = ((whole_sum + extra_term) / counts[:, None, :, None]).astype(jnp.bfloat16)
    return landmarks


def conv_apply(padded, tap_weights, row_count):
    conv_sum = jnp.zeros((padded.shape[0], row_count, padded.shape[2]), jnp.float32)
    for tap_index in range(tap_weights.shape[1]):
        conv_sum = (
            conv_sum + tap_weights[:, tap_index] * padded[:, tap_index : tap_index + row_count]
        )
    return conv_sum


def pack_vectors(vectors, device_total):
    flat_vec = jnp.concatenate(vectors)
    padding = -flat_vec.shape[0] % device_total
    return jnp.pad(flat_vec, (0, padding))


def unpack_vectors(flat_vec, piece_sizes):
    pieces = []
    offset = 0
    for length_val in piece_sizes:
        pieces.append(flat_vec[offset : offset + length_val])
        offset = offset + length_val
    return pieces


def body(
    hidden_in,
    seg_bounds,
    qkv_weight,
    query_bias,
    value_bias,
    conv_taps,
    out_weight,
    out_bias,
    first_gain,
    first_shift,
    up_weight,
    up_bias,
    down_weight,
    down_bias,
    second_gain,
    second_shift,
    grad_out,
):
    seq_count, tok_count, model_width = hidden_in.shape
    head_count, tap_count = conv_taps.shape
    head_width = model_width // head_count
    ff_width = up_weight.shape[1]
    seg_count = seg_bounds.shape[1] - 1
    halo_width = (tap_count - 1) // 2
    quarter = float(head_width) ** (-0.25)
    row_total = seq_count * tok_count
    device_total = lax.axis_size("batch") * lax.axis_size("seq")
    position = lax.axis_index("seq") * tok_count + jnp.arange(tok_count, dtype=jnp.int32)
    valid_mask = (position[None, :] < seg_bounds[:, seg_count:]).astype(jnp.float32)
    member = (
        (position[None, None, :] >= seg_bounds[:, :seg_count, None])
        & (position[None, None, :] < seg_bounds[:, 1:, None])
    ).astype(jnp.bfloat16)
    counts = (seg_bounds[:, 1:] - seg_bounds[:, :seg_count]).astype(jnp.float32)
    input_rows = hidden_in.reshape(row_total, model_width)
    bias_qkv = jnp.concatenate([query_bias, jnp.zeros_like(query_bias), value_bias])
    qkv_rows = (
        jnp.dot(input_rows, qkv_weight, preferred_element_type=jnp.float32) + bias_qkv
    ).reshape(seq_count, tok_count, 3 * model_width)
    queries = (qkv_rows[..., :model_width] * quarter).astype(jnp.bfloat16)
    key_rows = (qkv_rows[..., model_width : 2 * model_width] * quarter).astype(jnp.bfloat16)
    values = (qkv_rows[..., 2 * model_width :] * valid_mask[..., None]).astype(jnp.bfloat16)
    query_sums = jnp.einsum("smt,std->smd", member, queries, preferred_element_type=jnp.float32)
    key_sums = jnp.einsum("smt,std->smd", member, key_rows, preferred_element_type=jnp.float32)
    land_sums = jnp.stack([query_sums, key_sums], axis=1)
    landmarks = landmark_total(land_sums, jnp.zeros_like(land_sums), counts)
    land_query = landmarks[:, 0].reshape(seq_count, seg_count, head_count, head_width)
    land_key = landmarks[:, 1].reshape(seq_count, seg_count, head_count, head_width)
    split_q = heads_split(queries, head_count)
    split_k = heads_split(key_rows, head_count)
    split_v = heads_split(values, head_count)
    first_score = jnp.einsum(
        "sthe,smhe->shmt", split_q, land_key, preferred_element_type=jnp.float32
    )
    kernel_one = jax.nn.softmax(first_score, axis=2)
    kernel_low = kernel_one.astype(jnp.bfloat16)
    third_score = jnp.einsum(
        "smhe,sthe->shmt", land_query, split_k, preferred_element_type=jnp.float32
    )
    third_score = jnp.where(valid_mask[:, None, None, :] > 0.5, third_score, -1e30)
    score_top = lax.pmax(jnp.max(third_score, axis=-1), "seq")
    expo_val = jnp.exp(third_score - score_top[..., None])
    expo_low = expo_val.astype(jnp.bfloat16)
    acc_part = jnp.einsum("shmt,sthe->shme", expo_low, split_v, preferred_element_type=jnp.float32)
    acc_sum, exp_total = lax.psum((acc_part, jnp.sum(expo_val, axis=-1)), "seq")
    kv_mean = acc_sum / exp_total[..., None]
    mixed_val, mix_back, proxy_vals = jax.vjp(
        solve_mix,
        land_query.astype(jnp.float32),
        land_key.astype(jnp.float32),
        kv_mean,
        has_aux=True,
    )
    mixed_low = mixed_val.astype(jnp.bfloat16)
    attn_out = jnp.einsum(
        "shmt,shme->sthe", kernel_low, mixed_low, preferred_element_type=jnp.float32
    ).reshape(seq_count, tok_count, model_width)
    tap_weights = jnp.repeat(conv_taps, head_width, axis=0)
    padded_values = with_halo(values, (("seq", 1),), halo_width)
    branch = (
        (attn_out + conv_apply(padded_values, tap_weights, tok_count))
        .astype(jnp.bfloat16)
        .reshape(row_total, model_width)
    )
    first_sum = (
        input_rows.astype(jnp.float32)
        + jnp.dot(branch, out_weight, preferred_element_type=jnp.float32)
        + out_bias
    )
    normed_one, inv_one = layer_norm(first_sum)
    mid_rows = normed_one * first_gain + first_shift
    mid_low = mid_rows.astype(jnp.bfloat16)
    up_pre = jnp.dot(mid_low, up_weight, preferred_element_type=jnp.float32) + up_bias
    act_val, gelu_back = jax.vjp(partial(jax.nn.gelu, approximate=False), up_pre)
    act_low = act_val.astype(jnp.bfloat16)
    second_sum = (
        mid_rows + jnp.dot(act_low, down_weight, preferred_element_type=jnp.float32) + down_bias
    )
    normed_two, inv_two = layer_norm(second_sum)
    layer_out = (
        (normed_two * second_gain + second_shift)
        .astype(jnp.bfloat16)
        .reshape(seq_count, tok_count, model_width)
    )
    grad_rows = grad_out.reshape(row_total, model_width).astype(jnp.float32)
    second_gain_grad = jnp.sum(grad_rows * normed_two, axis=0)
    second_shift_grad = jnp.sum(grad_rows, axis=0)
    grad_second = norm_back(grad_rows * second_gain, normed_two, inv_two)
    grad_down = grad_second.astype(jnp.bfloat16)
    down_weight_grad = jnp.einsum(
        "nf,nd->fd", act_low, grad_down, preferred_element_type=jnp.float32
    )
    down_bias_grad = jnp.sum(grad_down.astype(jnp.float32), axis=0)
    (grad_up_val,) = gelu_back(
        jnp.einsum("nd,fd->nf", grad_down, down_weight, preferred_element_type=jnp.float32)
    )
    grad_up = grad_up_val.astype(jnp.bfloat16)
    up_weight_grad = jnp.einsum("nd,nf->df", mid_low, grad_up, preferred_element_type=jnp.float32)
    up_bias_grad = jnp.sum(grad_up.astype(jnp.float32), axis=0)
    grad_mid = grad_second + jnp.einsum(
        "nf,df->nd", grad_up, up_weight, preferred_element_type=jnp.float32
    )
    first_gain_grad = jnp.sum(grad_mid * normed_one, axis=0)
    first_shift_grad = jnp.sum(grad_mid, axis=0)
    ffn_pack = pack_vectors(
        [up_bias_grad, down_bias_grad, second_gain_grad, second_shift_grad], device_total
    )
    grad_first = norm_back(grad_mid * first_gain, normed_one, inv_one)
    grad_proj = grad_first.astype(jnp.bfloat16)
    out_weight_grad = jnp.einsum("nd,ne->de", branch, grad_proj, preferred_element_type=jnp.float32)
    out_bias_grad = jnp.sum(grad_proj.astype(jnp.float32), axis=0)
    grad_branch = (
        jnp.einsum("ne,de->nd", grad_proj, out_weight, preferred_element_type=jnp.float32)
        .astype(jnp.bfloat16)
        .reshape(seq_count, tok_count, model_width)
    )
    grad_heads = heads_split(grad_branch, head_count)
    grad_kernel = jnp.einsum(
        "sthe,shme->shmt", grad_heads, mixed_low, preferred_element_type=jnp.float32
    )
    grad_first_score = (
        kernel_one * (grad_kernel - jnp.sum(kernel_one * grad_kernel, axis=2, keepdims=True))
    ).astype(jnp.bfloat16)
    grad_mix_part = jnp.einsum(
        "shmt,sthe->shme", kernel_low, grad_heads, preferred_element_type=jnp.float32
    )
    grad_mixed = lax.psum(grad_mix_part, "seq")
    grad_lq_two, grad_lk_two, grad_kv = mix_back(grad_mixed)
    grad_query_one = jnp.einsum(
        "shmt,smhe->sthe", grad_first_score, land_key, preferred_element_type=jnp.float32
    )
    grad_lk_one = jnp.einsum(
        "shmt,sthe->smhe", grad_first_score, split_q, preferred_element_type=jnp.float32
    )
    grad_acc = (grad_kv / exp_total[..., None]).astype(jnp.bfloat16)
    grad_total = -jnp.sum(grad_kv * kv_mean, axis=-1) / exp_total
    grad_expo = (
        jnp.einsum("shme,sthe->shmt", grad_acc, split_v, preferred_element_type=jnp.float32)
        + grad_total[..., None]
    )
    grad_third = (expo_val * grad_expo).astype(jnp.bfloat16)
    grad_value_att = jnp.einsum(
        "shmt,shme->sthe", expo_low, grad_acc, preferred_element_type=jnp.float32
    )
    grad_key_three = jnp.einsum(
        "shmt,smhe->sthe", grad_third, land_query, preferred_element_type=jnp.float32
    )
    grad_lq_three = jnp.einsum(
        "shmt,sthe->smhe", grad_third, split_k, preferred_element_type=jnp.float32
    )
    grad_parts = jnp.stack(
        [
            grad_lq_three.reshape(seq_count, seg_count, model_width),
            grad_lk_one.reshape(seq_count, seg_count, model_width),
        ],
        axis=1,
    )
    grad_extra = jnp.stack(
        [
            grad_lq_two.reshape(seq_count, seg_count, model_width),
            grad_lk_two.reshape(seq_count, seg_count, model_width),
        ],
        axis=1,
    )
    grad_land = landmark_total(grad_parts, grad_extra, counts)
    padded_grad = with_halo(grad_branch, (("seq", 1),), halo_width)
    grad_values = grad_value_att.reshape(seq_count, tok_count, model_width) + conv_apply(
        padded_grad, tap_weights[:, ::-1], tok_count
    )
    grad_branch_wide = grad_branch.astype(jnp.float32)
    tap_grads = jnp.stack(
        [
            jnp.sum(
                grad_branch_wide * padded_values[:, tap_index : tap_index + tok_count], axis=(0, 1)
            )
            for tap_index in range(tap_count)
        ]
    )
    conv_grad = jnp.transpose(
        jnp.sum(tap_grads.reshape(tap_count, head_count, head_width), axis=-1)
    )
    grad_queries = (
        jnp.einsum("smt,smd->std", member, grad_land[:, 0], preferred_element_type=jnp.float32)
        + grad_query_one.reshape(seq_count, tok_count, model_width)
    ) * quarter
    grad_keys = (
        jnp.einsum("smt,smd->std", member, grad_land[:, 1], preferred_element_type=jnp.float32)
        + grad_key_three.reshape(seq_count, tok_count, model_width)
    ) * quarter
    grad_qkv = (
        jnp.concatenate([grad_queries, grad_keys, grad_values * valid_mask[..., None]], axis=-1)
        .astype(jnp.bfloat16)
        .reshape(row_total, 3 * model_width)
    )
    qkv_grad = jnp.einsum("nd,ne->de", input_rows, grad_qkv, preferred_element_type=jnp.float32)
    bias_cols = jnp.sum(grad_qkv.astype(jnp.float32), axis=0)
    query_bias_grad = bias_cols[:model_width]
    value_bias_grad = bias_cols[2 * model_width :]
    input_grad = (
        (
            grad_first
            + jnp.einsum("ne,de->nd", grad_qkv, qkv_weight, preferred_element_type=jnp.float32)
        )
        .astype(jnp.bfloat16)
        .reshape(seq_count, tok_count, model_width)
    )
    proxy_local = jnp.sum(proxy_vals, axis=0)
    attn_pack = pack_vectors(
        [
            query_bias_grad,
            value_bias_grad,
            conv_grad.reshape(-1),
            out_bias_grad,
            first_gain_grad,
            first_shift_grad,
            proxy_local,
        ],
        device_total,
    )
    share_tuple = (
        lax.psum_scatter(qkv_grad.reshape(-1), ("batch", "seq"), scatter_dimension=0, tiled=True),
        lax.psum_scatter(
            out_weight_grad.reshape(-1), ("batch", "seq"), scatter_dimension=0, tiled=True
        ),
        lax.psum_scatter(
            up_weight_grad.reshape(-1), ("batch", "seq"), scatter_dimension=0, tiled=True
        ),
        lax.psum_scatter(
            down_weight_grad.reshape(-1), ("batch", "seq"), scatter_dimension=0, tiled=True
        ),
        lax.psum_scatter(attn_pack, ("batch", "seq"), scatter_dimension=0, tiled=True),
        lax.psum_scatter(ffn_pack, ("batch", "seq"), scatter_dimension=0, tiled=True),
    )
    gathered = (
        lax.all_gather(share_tuple[0], ("batch", "seq"), axis=0, tiled=True),
        lax.all_gather(share_tuple[1], ("batch", "seq"), axis=0, tiled=True),
        lax.all_gather(share_tuple[2], ("batch", "seq"), axis=0, tiled=True),
        lax.all_gather(share_tuple[3], ("batch", "seq"), axis=0, tiled=True),
        lax.all_gather(share_tuple[4], ("batch", "seq"), axis=0, tiled=True),
        lax.all_gather(share_tuple[5], ("batch", "seq"), axis=0, tiled=True),
    )
    attn_small = unpack_vectors(
        gathered[4],
        [
            model_width,
            model_width,
            head_count * tap_count,
            model_width,
            model_width,
            model_width,
            head_count,
        ],
    )
    ffn_small = unpack_vectors(gathered[5], [ff_width, model_width, model_width, model_width])
    condition = attn_small[6] / (device_total * seq_count)
    return (
        layer_out,
        input_grad,
        gathered[0].reshape(model_width, 3 * model_width),
        attn_small[0],
        attn_small[1],
        attn_small[2].reshape(head_count, tap_count),
        gathered[1].reshape(model_width, model_width),
        attn_small[3],
        attn_small[4],
        attn_small[5],
        gathered[2].reshape(model_width, ff_width),
        ffn_small[0],
        gathered[3].reshape(ff_width, model_width),
        ffn_small[1],
        ffn_small[2],
        ffn_small[3],
        condition,
    )


def solution(mesh):
    placed = (
        P("batch", "seq", None),
        P("batch", None),
        P(),
        P(),
        P(),
        P(),
        P(),
        P(),
        P(),
        P(),
        P(),
        P(),
        P(),
        P(),
        P(),
        P(),
        P("batch", "seq", None),
    )
    return jax.shard_map(
        body,
        mesh=mesh,
        in_specs=placed,
        out_specs=(
            P("batch", "seq", None),
            P("batch", "seq", None),
            P(),
            P(),
            P(),
            P(),
            P(),
            P(),
            P(),
            P(),
            P(),
            P(),
            P(),
            P(),
            P(),
            P(),
            P(),
        ),
        check_vma=False,
    )
```

profile of v0, /device:TPU:0, one launch (start us, length us, event | category | flops | bytes accessed | tf_op | source)
XLA Modules:
  0.0 1281.5 jit_solution(8485358699621297553)
XLA Ops:
  14.8 5.4 collective-permute-start
  43.1 31.5 %all-reduce.18.cloned.1.call-done = f32[2,2,64,768]{3,2,0,1:T(8,128)} async-done(((f32[2,2,64,768]{3,2,0,1:T(8,128)}), f32[2,2,64,768]{3,2,0,1:T(8,128)}) %all-reduce.18.cloned.1.call-update) | async-done | bytes 786448 | tf_op jit(solution)/shard_map/psum | solution.py:76
  119.8 16.3 %pmax.7 = f32[2,12,64]{2,1,0:T(8,128)} all-reduce(f32[2,12,64]{2,1,0:T(8,128)} %get-tuple-element.134), channel_id=1, replica_groups=mesh['batch'=8,'seq'=4] {'seq'}, use_global_device_ids=true, to_apply=%region_5.6 | all-reduce | flops 1536 | bytes 12288 | tf_op jit(solution)/shard_map/pmax | solution.py:166
  141.6 15.4 %psum.37 = f32[2,12,64]{2,1,0:T(8,128)} all-reduce(f32[2,12,64]{2,1,0:T(8,128)} %fusion.127), channel_id=1, replica_groups=mesh['batch'=8,'seq'=4] {'seq'}, use_global_device_ids=true, to_apply=%region_8.9 | all-reduce | flops 1536 | bytes 12288 | tf_op jit(solution)/shard_map/psum | solution.py:170
  157.0 4.0 fusion.261
  161.0 27.1 %all-reduce.20.cloned.1.call-done = f32[2,12,64,64]{3,2,1,0:T(8,128)} async-done(((f32[2,12,64,64]{3,2,1,0:T(8,128)}), f32[2,12,64,64]{3,2,1,0:T(8,128)}) %all-reduce.20.cloned.1.call-update) | async-done | bytes 393232 | tf_op jit(solution)/shard_map/psum | solution.py:170
  198.1 26.3 %fusion.47 = bf16[2,256,768]{2,1,0:T(8,128)(2,1)S(1)} fusion(f32[2,256,768]{2,1,0:T(8,128)} %copy.214, bf16[2,256,768]{2,1,0:T(8,128)(2,1)} %copy-done.5, bf16[2,16,768]{2,1,0:T(8,128)(2,1)} %collective-permute-done.1, bf16[2,16,768]{2,1,0:T(8,128)(2,1)} %collective-permute-done, f32[768]{0:T(1024)} %get-tuple-element.59, f32[768]{0:T(1024)} %get-tuple-element.60, ...), kind=kLoop, calls=%fused_computation.191 | loop fusion | flops 77070336 | bytes 3345408 | tf_op jit(solution)/shard_map/convert_element_type | solution.py:187
  226.2 19.7 %multiply_convert_fusion = (bf16[512,3072]{1,0:T(8,128)(2,1)S(1)}, f32[512,3072]{1,0:T(8,128)}, f32[512,3072]{1,0:T(8,128)}) fusion(f32[3072]{0:T(1024)S(1)} %copy-done.141, bf16[768,3072]{1,0:T(8,128)(2,1)} %param.27, f32[512,768]{1,0:T(8,128)S(1)} %get-tuple-element.139, f32[768]{0:T(1024)S(1)} %copy-done.144, f32[768]{0:T(1024)S(1)} %copy-done.127, ...), kind=kOutput, calls=%fused_computation.40 | convolution fusion | flops 2521694208 | bytes 22042624 | tf_op jit(solution)/shard_map/dot_general | solution.py:198
  253.2 9.9 convert_reduce_fusion
  263.1 5.7 multiply_reduce_fusion
  270.0 5.7 fusion.81
  294.1 5.5 convolution_bitcast_fusion.1
  314.8 9.8 copy.290
  324.6 5.2 fusion.236
  329.8 11.0 reshape.444
  340.8 15.9 %all-reduce.22.cloned.1.call-done = f32[2,12,64,64]{3,2,1,0:T(8,128)} async-done(((f32[2,12,64,64]{3,2,1,0:T(8,128)}), f32[2,12,64,64]{3,2,1,0:T(8,128)}) %all-reduce.22.cloned.1.call-update) | async-done | bytes 393232 | tf_op jit(solution)/shard_map/psum | solution.py:252
  449.5 27.3 %multiply_convert_fusion.1 = bf16[2,256,768]{2,1,0:T(8,128)(2,1)} fusion(f32[2,256,768]{2,1,0:T(8,128)} %copy.251, bf16[2,256,768]{2,1,0:T(8,128)(2,1)} %bitcast.289, bf16[2,16,768]{2,1,0:T(8,128)(2,1)} %collective-permute-done.3, bf16[2,16,768]{2,1,0:T(8,128)(2,1)} %collective-permute-done.2, f32[768]{0:T(1024)} %get-tuple-element.59, ...), kind=kLoop, calls=%fused_computation.264 | loop fusion | flops 77463552 | bytes 3347456 | tf_op jit(solution)/shard_map/convert.7
  493.1 5.1 all-reduce.24.cloned.1.call-done
  503.3 5.0 convolution_bitcast_fusion
  508.3 8.0 copy.253
  516.3 7.9 reshape.436
  524.3 432.3 %all-reduce.26.cloned.1.call-done = (f32[1769472]{0:T(1024)}, f32[589824]{0:T(1024)}, f32[2359296]{0:T(1024)}, f32[2359296]{0:T(1024)}) async-done(((f32[1769472]{0:T(1024)}, f32[589824]{0:T(1024)}, f32[2359296]{0:T(1024)}, f32[2359296]{0:T(1024)}), (f32[1769472]{0:T(1024)}, f32[589824]{0:T(1024)}, f32[2359296]{0:T(1024)}, f32[2359296]{0:T(1024)})) %all-reduce.26.cloned.1.call-update) | async-done | bytes 28311568
  963.5 5.4 fusion.80
  987.6 6.3 fusion.97
  994.7 6.8 fusion.98
  1073.0 41.6 %all-reduce.10 = (f32[4256]{0:T(1024)}, f32[5376]{0:T(1024)}) all-reduce(f32[4256]{0:T(1024)} %pad.4, f32[5376]{0:T(1024)} %pad_maximum_fusion.8), channel_id=3, replica_groups=mesh['batch'=8,'seq'=4] {'batch','seq'}, use_global_device_ids=true, to_apply=%region_66.67.clone | all-reduce | flops 9632 | bytes 77056
  1118.7 42.2 %all-reduce.9 = (f32[4256]{0:T(1024)}, f32[5376]{0:T(1024)}) all-reduce(f32[4256]{0:T(1024)} %dynamic-slice_dynamic-update-slice_fusion.1, f32[5376]{0:T(1024)} %dynamic-slice_dynamic-update-slice_fusion), channel_id=1, replica_groups=mesh['batch'=8,'seq'=4] {'batch','seq'}, use_global_device_ids=true, to_apply=%add.1 | all-reduce | flops 9632 | bytes 77056
  1167.7 5.0 add_convert_fusion.1
  1176.2 8.2 reshape.437
  1184.5 11.3 reshape.445
  1195.8 68.1 %all-gather.9.cloned.1.call-done = f32[2359296]{0:T(1024)} async-done(((f32[73728]{0:T(1024)}), f32[2359296]{0:T(1024)}) %all-gather.9.cloned.1.call-update) | async-done | bytes 9437200 | tf_op jit(solution)/shard_map/all_gather | solution.py:362
  1263.8 10.9 reshape.443
  (584 shorter events, 359.2 us)
Async XLA Ops:
  7.2 67.4 %all-reduce.18.cloned.1.call-start = ((), (), s32[]{:S(2)}) async-start(), calls=%async_computation | async-start | bytes 1572864 | tf_op jit(solution)/shard_map/psum | solution.py:76
  7.3 14.7 %copy-start.114 = (s32[256]{0:T(256)}, s32[256]{0:T(256)S(1)}, u32[]{:S(2)}) copy-start(s32[256]{0:T(256)S(1)} %iota_add_fusion) | copy-start | bytes 3076
  14.8 183.2 %collective-permute-start = (bf16[2,16,768]{2,1,0:T(8,128)(2,1)}, bf16[2,16,768]{2,1,0:T(8,128)(2,1)}, u32[]{:S(2)}, u32[]{:S(2)}) collective-permute-start(bf16[2,16,768]{2,1,0:T(8,128)(2,1)} %get-tuple-element.111), channel_id=1, source_target_pairs={{0,1},{1,2},{2,3},{4,5},{5,6},{6,7},{8,9},{9,10},{10,11},{12,13},{... | collective-permute-start | bytes 147464 | tf_op jit(solution)/shard_map/ppermute | solution.py:23
  20.3 177.8 %collective-permute-start.1 = (bf16[2,16,768]{2,1,0:T(8,128)(2,1)}, bf16[2,16,768]{2,1,0:T(8,128)(2,1)}, u32[]{:S(2)}, u32[]{:S(2)}) collective-permute-start(bf16[2,16,768]{2,1,0:T(8,128)(2,1)} %get-tuple-element.112), channel_id=1, source_target_pairs={{1,0},{2,1},{3,2},{5,4},{6,5},{7,6},{9,8},{10,9},{11,10},{13,12},{... | collective-permute-start | bytes 147464 | tf_op jit(solution)/shard_map/ppermute | solution.py:25
  21.6 52.9 %copy-start.121 = (f32[2,64]{1,0:T(2,128)}, f32[2,64]{1,0:T(2,128)S(1)}, u32[]{:S(2)}) copy-start(f32[2,64]{1,0:T(2,128)S(1)} %get-tuple-element.129) | copy-start | bytes 1540
  23.3 164.8 %all-reduce.20.cloned.1.call-start = ((), (), s32[]{:S(2)}) async-start(), calls=%async_computation.1 | async-start | bytes 1572864 | tf_op jit(solution)/shard_map/psum | solution.py:170
  83.2 26.3 %copy-start.1 = (f32[2,12,64,64]{2,3,1,0:T(8,128)}, f32[2,12,64,64]{2,3,1,0:T(8,128)S(1)}, u32[]{:S(2)}) copy-start(f32[2,12,64,64]{2,3,1,0:T(8,128)S(1)} %get-tuple-element.133) | copy-start | bytes 1179652
  84.1 30.8 %copy-start.129 = (f32[2,12]{1,0:T(2,128)}, f32[2,12]{1,0:T(2,128)S(1)}, u32[]{:S(2)}) copy-start(f32[2,12]{1,0:T(2,128)S(1)} %multiply_reduce_fusion.9) | copy-start | bytes 292
  139.0 217.7 %all-reduce.22.cloned.1.call-start = ((), (), s32[]{:S(2)}) async-start(), calls=%async_computation.2 | async-start | bytes 1572864 | tf_op jit(solution)/shard_map/psum | solution.py:252
  198.1 26.3 %copy-start.136 = (bf16[768,768]{1,0:T(8,128)(2,1)S(1)}, bf16[768,768]{1,0:T(8,128)(2,1)}, u32[]{:S(2)}) copy-start(bf16[768,768]{1,0:T(8,128)(2,1)} %param.23) | copy-start | bytes 3538948
  198.1 26.3 %copy-start.137 = (bf16[2,256,768]{2,1,0:T(8,128)(2,1)S(1)}, bf16[2,256,768]{2,1,0:T(8,128)(2,1)}, u32[]{:S(2)}) copy-start(bf16[2,256,768]{2,1,0:T(8,128)(2,1)} %param.17) | copy-start | bytes 2359300
  198.1 26.3 %copy-start.142 = (f32[768]{0:T(1024)S(1)}, f32[768]{0:T(1024)}, u32[]{:S(2)}) copy-start(f32[768]{0:T(1024)} %param.24) | copy-start | bytes 9220
  198.1 47.8 %slice-start = ((s8[4718592]{0:T(1024)(128)(4,1)}), s8[4194304]{0:T(1024)(128)(4,1)S(1)}, s32[]{:S(2)}) async-start(s8[4718592]{0:T(1024)(128)(4,1)} %bitcast.322), calls=%async_computation.9 | async-start | bytes 8388608
  225.3 43.5 %copy-start.75 = (f32[512,768]{1,0:T(8,128)}, f32[512,768]{1,0:T(8,128)S(1)}, u32[]{:S(2)}) copy-start(f32[512,768]{1,0:T(8,128)S(1)} %get-tuple-element.139) | copy-start | bytes 4718596
  225.3 43.5 %copy-start.116 = (f32[512]{0:T(512)}, f32[512]{0:T(512)S(1)}, u32[]{:S(2)}) copy-start(f32[512]{0:T(512)S(1)} %broadcast_multiply_fusion.4) | copy-start | bytes 6148
  226.1 42.7 %copy-start.124 = (f32[512]{0:T(512)}, f32[512]{0:T(512)S(1)}, u32[]{:S(2)}) copy-start(f32[512]{0:T(512)S(1)} %add_rsqrt_fusion.1) | copy-start | bytes 6148
  226.1 19.7 %slice-start.1 = ((s8[4718592]{0:T(1024)(128)(4,1)}), s8[524288]{0:T(1024)(128)(4,1)S(1)}, s32[]{:S(2)}) async-start(s8[4718592]{0:T(1024)(128)(4,1)} %bitcast.322), calls=%async_computation.10 | async-start | bytes 1048576
  226.1 19.7 %copy-start.143 = (f32[768]{0:T(1024)S(1)}, f32[768]{0:T(1024)}, u32[]{:S(2)}) copy-start(f32[768]{0:T(1024)} %param.30) | copy-start | bytes 9220
  251.1 12.1 slice-start.2
  301.1 148.3 %collective-permute-start.2 = (bf16[2,16,768]{2,1,0:T(8,128)(2,1)}, bf16[2,16,768]{2,1,0:T(8,128)(2,1)}, u32[]{:S(2)}, u32[]{:S(2)}) collective-permute-start(bf16[2,16,768]{2,1,0:T(8,128)(2,1)} %get-tuple-element.109), channel_id=1, source_target_pairs={{0,1},{1,2},{2,3},{4,5},{5,6},{6,7},{8,9},{9,10},{10,11},{12,13},{... | collective-permute-start | bytes 147464 | tf_op jit(solution)/shard_map/ppermute | solution.py:23
  305.1 144.4 %collective-permute-start.3 = (bf16[2,16,768]{2,1,0:T(8,128)(2,1)}, bf16[2,16,768]{2,1,0:T(8,128)(2,1)}, u32[]{:S(2)}, u32[]{:S(2)}) collective-permute-start(bf16[2,16,768]{2,1,0:T(8,128)(2,1)} %get-tuple-element.110), channel_id=1, source_target_pairs={{1,0},{2,1},{3,2},{5,4},{6,5},{7,6},{9,8},{10,9},{11,10},{13,12},{... | collective-permute-start | bytes 147464 | tf_op jit(solution)/shard_map/ppermute | solution.py:25
  306.4 191.9 %all-reduce.24.cloned.1.call-start = ((), (), s32[]{:S(2)}) async-start(), calls=%async_computation.3 | async-start | bytes 1572864 | tf_op jit(solution)/shard_map/psum | solution.py:76
  449.4 507.2 %all-reduce.26.cloned.1.call-start = ((), (), s32[]{:S(2)}) async-start(), calls=%async_computation.8 | async-start | bytes 56623104
  449.4 27.3 %copy-start.4 = (f32[2,12,64,64]{2,3,1,0:T(8,128)S(1)}, f32[2,12,64,64]{2,3,1,0:T(8,128)}, u32[]{:S(2)}) copy-start(f32[2,12,64,64]{2,3,1,0:T(8,128)} %copy-done.1) | copy-start | bytes 1179652
  449.4 27.3 %copy-start.81 = (bf16[2,1,64,768]{2,3,0,1:T(8,128)(2,1)S(1)}, bf16[2,1,64,768]{2,3,0,1:T(8,128)(2,1)}, u32[]{:S(2)}) copy-start(bf16[2,1,64,768]{2,3,0,1:T(8,128)(2,1)} %copy.287) | copy-start | bytes 589828
  449.4 27.3 %copy-start.120 = (f32[2,12,64]{2,1,0:T(8,128)S(1)}, f32[2,12,64]{2,1,0:T(8,128)}, u32[]{:S(2)}) copy-start(f32[2,12,64]{2,1,0:T(8,128)} %neg.98) | copy-start | bytes 18436
  449.5 27.3 %copy-start.147 = (f32[2,12,64,64]{2,3,1,0:T(8,128)S(1)}, f32[2,12,64,64]{2,3,1,0:T(8,128)}, u32[]{:S(2)}) copy-start(f32[2,12,64,64]{2,3,1,0:T(8,128)} %get-tuple-element.153) | copy-start | bytes 1179652
  524.2 439.2 %copy-start.132 = (f32[768]{0:T(1024)S(1)}, f32[768]{0:T(1024)}, u32[]{:S(2)}) copy-start(f32[768]{0:T(1024)} %get-tuple-element.37) | copy-start | bytes 9220
  524.2 648.5 %all-gather.7.cloned.1.call-start = ((), (), s32[]{:S(2)}) async-start(), calls=%async_computation.5 | async-start | bytes 2433024 | tf_op jit(solution)/shard_map/all_gather | solution.py:361
  958.1 218.1 %all-gather.5.cloned.1.call-start = ((), (), s32[]{:S(2)}) async-start(), calls=%async_computation.4 | async-start | bytes 7299072 | tf_op jit(solution)/shard_map/all_gather | solution.py:360
  959.9 224.6 %all-gather.11.cloned.1.call-start = ((), (), s32[]{:S(2)}) async-start(), calls=%async_computation.7 | async-start | bytes 9732096 | tf_op jit(solution)/shard_map/all_gather | solution.py:363
  961.6 302.2 %all-gather.9.cloned.1.call-start = ((), (), s32[]{:S(2)}) async-start(), calls=%async_computation.6 | async-start | bytes 9732096 | tf_op jit(solution)/shard_map/all_gather | solution.py:362
  (133 other events, 330.7 us)
Sparse Core Ops, SparseCore 0:
  23.4 51.1 all-reduce.17
  139.1 48.9 all-reduce.19
  306.5 50.1 all-reduce.21
  449.5 48.7 all-reduce.23
  524.4 432.2 all-reduce.25
  959.8 57.3 all-gather.6
  1021.1 72.0 all-gather.4
  1097.0 82.1 all-gather.10
  1183.1 80.6 all-gather.8
where the time goes:
time: 1290 us; the launch traced here: 1280 us
  waiting for transfers between devices  580 us (45%)
  local copies, waits for them, and re-layouts  241 us (19%)
  matrix products  211 us (16%)
  blocking collectives  116 us (9%)
  other arithmetic  105 us (8%)
  between operations  16.4 us (1%)
    unnamed x10, waiting for transfers between devices  432 us
    unnamed x2, blocking collectives  83.8 us
    unnamed x347, local copies, waits for them, and re-layouts  74.5 us
    all_gather x1, waiting for transfers between devices, body(): lax.all_gather(share_tuple[2], ('batch', 'seq'), axis=0, tiled=True)  68.1 us
    dot_general x36, matrix products, pseudo_inverse(): jnp.matmul(product, inner_term, precision=precise)  47.6 us
    another operation x34, local copies, waits for them, and re-layouts, body(): jnp.stack([jnp.sum(grad_branch_wide * padded_values[:, tap_index:tap_inde...  42.4 us
    psum x2, waiting for transfers between devices, landmark_total(): whole_sum = lax.psum(partial_sum, 'seq')  36.6 us
    dot_general x18, matrix products, pseudo_inverse(): product = jnp.matmul(kernel, approx, precision=precise)  27.4 us
  transfers between devices with their start and end apart: 13, of which 6 were waited for; matrix products, arithmetic and copies ran while one was open for 31% of the time, Pallas kernels for 0%

commit v1 on v0

--- a/solution.py
+++ b/solution.py
@@ -1,11 +1,403 @@
+import math
 from functools import partial
 
 import jax
 import jax.numpy as jnp
 from jax import lax
+from jax.experimental import pallas as pl
+from jax.experimental.pallas import tpu as pltpu
 from jax.sharding import PartitionSpec as P
 
 NEWTON = 6
+
+MESH_IDS = pl.DeviceIdType.MESH
+HALF = 384
+LANES = 128
+
+
+def plane_sides(count):
+    wide = max(d for d in range(1, math.isqrt(count) + 1) if count % d == 0)
+    return wide, count // wide
+
+
+class Place:
+    def __init__(self, batch_size, seq_size):
+        x_size, y_size = plane_sides(seq_size)
+        self.sizes = {"core": 2, "x": x_size, "y": y_size, "z": batch_size // 2}
+        batch = lax.axis_index("batch")
+        seq = lax.axis_index("seq")
+        self.at = {
+            "core": lax.rem(batch, 2),
+            "z": lax.div(batch, 2),
+            "x": lax.rem(seq, x_size),
+            "y": lax.div(seq, x_size),
+        }
+        self.seq_size = seq_size
+        self.seq = seq
+        self.batch = batch
+
+    def peer_index(self, axis, step):
+        size = self.sizes[axis]
+        return lax.rem(self.at[axis] + step, size)
+
+    def device(self, **moved):
+        spot = {**self.at, **moved}
+        return (spot["z"] * 2 + spot["core"], spot["y"] * self.sizes["x"] + spot["x"])
+
+    def peers(self, axes):
+        for axis in axes:
+            for step in range(1, self.sizes[axis]):
+                yield self.device(**{axis: self.peer_index(axis, step)})
+
+    def seq_peer(self, step):
+        return (self.batch, lax.rem(self.seq + step, self.seq_size))
+
+
+def greet(devices):
+    barrier = pltpu.get_barrier_semaphore()
+    devices = list(devices)
+    for device in devices:
+        pl.semaphore_signal(barrier, inc=1, device_id=device, device_id_type=MESH_IDS)
+    return lambda: pl.semaphore_wait(barrier, len(devices))
+
+
+def tile_rows(rows):
+    return max(t for t in (96, 64, 48, 32, 16) if rows % t == 0)
+
+
+def add_rows(out_ref, in_ref, at, parts, rows):
+    tile = tile_rows(rows)
+
+    def step(index, carry):
+        start = pl.multiple_of(at + index * tile, 16)
+        total = in_ref[pl.ds(start, tile), :].astype(jnp.float32)
+        for ref, first in parts:
+            total = total + ref[pl.ds(pl.multiple_of(first + index * tile, 16), tile), :].astype(
+                jnp.float32
+            )
+        out_ref[pl.ds(start, tile), :] = total.astype(out_ref.dtype)
+        return carry
+
+    lax.fori_loop(0, rows // tile, step, 0)
+
+
+class Reduce:
+    ORDERS = (("x", "y", "z"), ("y", "x", "z"))
+
+    def __init__(self, place, stage, whole, recv, send_sem, recv_sem, free_sem, rows):
+        self.place, self.stage, self.whole, self.recv = place, stage, whole, recv
+        self.send_sem, self.recv_sem, self.rows = send_sem, recv_sem, rows
+        self.free_sem = free_sem
+        self.sem = 0
+        self.mine = stage.at[place.at["core"]]
+        self.levels = []
+        for half, order in enumerate(self.ORDERS):
+            base, size, slot, levels = half * (rows // 2), rows // 2, 0, []
+            for axis in order:
+                count = place.sizes[axis]
+                chunk = size // count
+                levels.append((axis, count, base, chunk, slot))
+                slot += (count - 1) * chunk
+                base = base + place.at[axis] * chunk
+                size = chunk
+            self.levels.append(levels)
+
+    @staticmethod
+    def slots(sizes, rows):
+        need = []
+        for order in Reduce.ORDERS:
+            size, slot = rows // 2, 0
+            for axis in order:
+                size //= sizes[axis]
+                slot += (sizes[axis] - 1) * size
+            need.append(slot)
+        return max(need)
+
+    @staticmethod
+    def copies(sizes):
+        return 2 * (1 + 2 * sum(sizes[a] - 1 for a in ("x", "y", "z")))
+
+    def copy(self, src, dst, device):
+        index = self.sem
+        self.sem += 1
+        return pltpu.make_async_remote_copy(
+            src_ref=src,
+            dst_ref=dst,
+            send_sem=self.send_sem.at[index],
+            recv_sem=self.recv_sem.at[index],
+            device_id=device,
+            device_id_type=MESH_IDS,
+        )
+
+    @staticmethod
+    def rows_of(ref, start, rows):
+        return ref.at[pl.ds(pl.multiple_of(start, 16), rows)]
+
+    def scatter(self, half, level):
+        axis, count, base, chunk, slot = self.levels[half][level]
+        copies = []
+        for step in range(1, count):
+            peer = self.place.peer_index(axis, step)
+            copies.append(
+                self.copy(
+                    self.rows_of(self.mine, base + peer * chunk, chunk),
+                    self.recv.at[half, pl.ds(slot + (step - 1) * chunk, chunk)],
+                    self.place.device(**{axis: peer}),
+                )
+            )
+        return copies
+
+    def add_level(self, half, level):
+        axis, count, base, chunk, slot = self.levels[half][level]
+        add_rows(
+            self.whole if level == 2 else self.mine,
+            self.mine,
+            base + self.place.at[axis] * chunk,
+            [(self.recv.at[half], slot + k * chunk) for k in range(count - 1)],
+            chunk,
+        )
+
+    def run(self):
+        place, rows = self.place, self.rows
+        core = place.at["core"]
+        out = self.copy(
+            self.stage.at[1 - core], self.whole, place.device(core=1 - core)
+        )
+        out.start()
+        yield
+        out.wait()
+        pl.semaphore_signal(
+            self.free_sem, inc=1, device_id=place.device(core=1 - core), device_id_type=MESH_IDS
+        )
+        pending = []
+        for half in range(2):
+            add_rows(
+                self.mine,
+                self.mine,
+                half * (rows // 2),
+                [(self.whole, half * (rows // 2))],
+                rows // 2,
+            )
+            copies = self.scatter(half, 0)
+            for copy in copies:
+                copy.start()
+            pending.append(copies)
+        for level in range(3):
+            yield
+            later = []
+            for half in range(2):
+                for copy in pending[half]:
+                    copy.wait()
+                self.add_level(half, level)
+                copies = self.scatter(half, level + 1) if level < 2 else self.spread(half, 2)
+                for copy in copies:
+                    copy.start()
+                later.append(copies)
+            pending = later
+        for level in (2, 1, 0):
+            yield
+            later = []
+            for half in range(2):
+                for copy in pending[half]:
+                    copy.wait()
+                if level:
+                    copies = self.spread(half, level - 1)
+                    for copy in copies:
+                        copy.start()
+                    later.append(copies)
+            pending = later
+        pl.semaphore_wait(self.free_sem, 1)
+        out = self.copy(self.whole, self.stage.at[core], place.device(core=1 - core))
+        out.start()
+        yield
+        out.wait()
+
+    def spread(self, half, level):
+        axis, count, base, chunk, slot = self.levels[half][level]
+        here = self.rows_of(self.whole, base + self.place.at[axis] * chunk, chunk)
+        return [
+            self.copy(here, here, self.place.device(**{axis: self.place.peer_index(axis, step)}))
+            for step in range(1, count)
+        ]
+
+
+def vec_reduce(place, acc, slots, send_sem, recv_sem):
+    sem = 0
+    level = 0
+    for axis in ("core", "x", "y", "z"):
+        count = place.sizes[axis]
+        copies = []
+        here = place.at[axis]
+        for step in range(1, count):
+            copies.append(
+                pltpu.make_async_remote_copy(
+                    src_ref=acc,
+                    dst_ref=slots.at[level + here],
+                    send_sem=send_sem.at[sem],
+                    recv_sem=recv_sem.at[sem],
+                    device_id=place.device(**{axis: place.peer_index(axis, step)}),
+                    device_id_type=MESH_IDS,
+                )
+            )
+            sem += 1
+        for copy in copies:
+            copy.start()
+        slots[level + here] = acc[...]
+        yield
+        for copy in copies:
+            copy.wait()
+        total = slots[level]
+        for index in range(1, count):
+            total = total + slots[level + index]
+        acc[...] = total
+        level += count
+
+
+def interleave(generators, offsets):
+    live = [(g, o) for g, o in zip(generators, offsets)]
+    step = 0
+    while live:
+        keep = []
+        for generator, offset in live:
+            if step < offset:
+                keep.append((generator, offset))
+                continue
+            try:
+                next(generator)
+                keep.append((generator, offset))
+            except StopIteration:
+                pass
+        live = keep
+        step += 1
+
+
+def grad_kernel(batch_size, seq_size, plan, rows, *refs):
+    arrays = refs[:4]
+    (
+        vec_in, out_ref, vec_out, stage, whole, recv, slots, copy_sem, send_sem, recv_sem,
+        free_sem, vsend, vrecv, out_sem,
+    ) = refs[4:]
+    place = Place(batch_size, seq_size)
+    wait_greet = greet(place.peers(("core", "x", "y", "z")))
+    fills = []
+    for piece, blocks in enumerate(plan):
+        fill = []
+        for spot, (array, row, col) in enumerate(blocks):
+            for core in range(2):
+                fill.append(
+                    pltpu.make_async_copy(
+                        arrays[array].at[pl.ds(row, 768), pl.ds(col + core * HALF, HALF)],
+                        stage.at[piece, core, pl.ds(spot * 768, 768)],
+                        copy_sem.at[piece, spot * 2 + core],
+                    )
+                )
+        for copy in fill:
+            copy.start()
+        fills.append(fill)
+    vec_out[...] = vec_in[...]
+    wait_greet()
+
+    def piece_run(piece):
+        for copy in fills[piece]:
+            copy.wait()
+        yield from Reduce(
+            place, stage.at[piece], whole.at[piece], recv.at[piece],
+            send_sem.at[piece], recv_sem.at[piece], free_sem.at[piece], rows,
+        ).run()
+        core = place.at["core"]
+        outs = [
+            pltpu.make_async_copy(
+                whole.at[piece], out_ref.at[piece, core], out_sem.at[piece, 0]
+            ),
+            pltpu.make_async_copy(
+                stage.at[piece, 1 - core], out_ref.at[piece, 1 - core], out_sem.at[piece, 1]
+            ),
+        ]
+        for out in outs:
+            out.start()
+        yield
+        for out in outs:
+            out.wait()
+
+    runs = [piece_run(p) for p in range(len(plan))]
+    runs.append(vec_reduce(place, vec_out, slots, vsend, vrecv))
+    interleave(runs, list(range(len(plan))) + [0])
+
+
+BLOCKS = (
+    (0, 0, 0), (0, 768, 0), (0, 1536, 0), (0, 2304, 0),
+    (1, 0, 0), (1, 0, 768), (1, 0, 1536), (1, 0, 2304),
+    (2, 0, 0), (3, 0, 0), (3, 0, 768), (3, 0, 1536),
+)
+
+
+def piece_plan(sizes):
+    unit = 32 * sizes["x"] * sizes["y"] * sizes["z"]
+    many = 2 if 1536 % unit == 0 else 4
+    return many, -(-many * 768 // unit) * unit
+
+
+def grad_reduce(down, up, out, qkv, vec, batch_size, seq_size):
+    x_size, y_size = plane_sides(seq_size)
+    sizes = {"core": 2, "x": x_size, "y": y_size, "z": batch_size // 2}
+    many, rows = piece_plan(sizes)
+    plan = [BLOCKS[i : i + many] for i in range(0, len(BLOCKS), many)]
+    pieces = len(plan)
+    copies = Reduce.copies(sizes)
+    vec_steps = sum(sizes[a] - 1 for a in sizes)
+    vec_slots = sum(sizes.values())
+    any_spec = pl.BlockSpec(memory_space=pl.ANY)
+    vmem = pl.BlockSpec(memory_space=pltpu.VMEM)
+    gathered, vec = pl.pallas_call(
+        partial(grad_kernel, batch_size, seq_size, plan, rows),
+        out_shape=(
+            jax.ShapeDtypeStruct((pieces, 2, rows, HALF), jnp.bfloat16),
+            jax.ShapeDtypeStruct(vec.shape, jnp.float32),
+        ),
+        in_specs=[any_spec] * 4 + [vmem],
+        out_specs=(any_spec, vmem),
+        scratch_shapes=[
+            pltpu.VMEM((pieces, 2, rows, HALF), jnp.bfloat16),
+            pltpu.VMEM((pieces, rows, HALF), jnp.bfloat16),
+            pltpu.VMEM((pieces, 2, Reduce.slots(sizes, rows), HALF), jnp.bfloat16),
+            pltpu.VMEM((vec_slots, *vec.shape), jnp.float32),
+            pltpu.SemaphoreType.DMA((pieces, 2 * many)),
+            pltpu.SemaphoreType.DMA((pieces, copies)),
+            pltpu.SemaphoreType.DMA((pieces, copies)),
+            pltpu.SemaphoreType.REGULAR((pieces,)),
+            pltpu.SemaphoreType.DMA((vec_steps,)),
+            pltpu.SemaphoreType.DMA((vec_steps,)),
+            pltpu.SemaphoreType.DMA((pieces, 2)),
+        ],
+        compiler_params=pltpu.CompilerParams(
+            collective_id=0, has_side_effects=True, vmem_limit_bytes=58 * 2**20
+        ),
+        name="grad_reduce",
+    )(down, up, out, qkv, vec)
+    return many, gathered, vec
+
+
+def widen_kernel(in_ref, out_ref):
+    out_ref[...] = in_ref[0, 0].astype(jnp.float32)
+
+
+def widen(gathered, many, first, shape):
+    down_way = shape[0] > shape[1]
+    count = shape[0] // 768 * (shape[1] // 768)
+    return pl.pallas_call(
+        widen_kernel,
+        out_shape=jax.ShapeDtypeStruct(shape, jnp.float32),
+        grid=(count, 2),
+        in_specs=[
+            pl.BlockSpec(
+                (1, 1, 768, HALF), lambda b, c: (lax.div(first + b, many), c, lax.rem(first + b, many), 0)
+            )
+        ],
+        out_specs=pl.BlockSpec(
+            (768, HALF), (lambda b, c: (b, c)) if down_way else (lambda b, c: (0, b * 2 + c))
+        ),
+        name="widen",
+    )(gathered)
 
 
 precise = lax.Precision.HIGHEST
@@ -87,10 +479,9 @@
     return conv_sum
 
 
-def pack_vectors(vectors, device_total):
+def pack_vectors(vectors):
     flat_vec = jnp.concatenate(vectors)
-    padding = -flat_vec.shape[0] % device_total
-    return jnp.pad(flat_vec, (0, padding))
+    return jnp.pad(flat_vec, (0, -flat_vec.shape[0] % 1024)).reshape(-1, 128)
 
 
 def unpack_vectors(flat_vec, piece_sizes):
@@ -129,7 +520,8 @@
     halo_width = (tap_count - 1) // 2
     quarter = float(head_width) ** (-0.25)
     row_total = seq_count * tok_count
-    device_total = lax.axis_size("batch") * lax.axis_size("seq")
+    batch_size, seq_size = lax.axis_size("batch"), lax.axis_size("seq")
+    device_total = batch_size * seq_size
     position = lax.axis_index("seq") * tok_count + jnp.arange(tok_count, dtype=jnp.int32)
     valid_mask = (position[None, :] < seg_bounds[:, seg_count:]).astype(jnp.float32)
     member = (
@@ -227,9 +619,6 @@
     )
     first_gain_grad = jnp.sum(grad_mid * normed_one, axis=0)
     first_shift_grad = jnp.sum(grad_mid, axis=0)
-    ffn_pack = pack_vectors(
-        [up_bias_grad, down_bias_grad, second_gain_grad, second_shift_grad], device_total
-    )
     grad_first = norm_back(grad_mid * first_gain, normed_one, inv_one)
     grad_proj = grad_first.astype(jnp.bfloat16)
     out_weight_grad = jnp.einsum("nd,ne->de", branch, grad_proj, preferred_element_type=jnp.float32)
@@ -330,8 +719,12 @@
         .reshape(seq_count, tok_count, model_width)
     )
     proxy_local = jnp.sum(proxy_vals, axis=0)
-    attn_pack = pack_vectors(
+    vector = pack_vectors(
         [
+            up_bias_grad,
+            down_bias_grad,
+            second_gain_grad,
+            second_shift_grad,
             query_bias_grad,
             value_bias_grad,
             conv_grad.reshape(-1),
@@ -339,34 +732,24 @@
             first_gain_grad,
             first_shift_grad,
             proxy_local,
-        ],
-        device_total,
-    )
-    share_tuple = (
-        lax.psum_scatter(qkv_grad.reshape(-1), ("batch", "seq"), scatter_dimension=0, tiled=True),
-        lax.psum_scatter(
-            out_weight_grad.reshape(-1), ("batch", "seq"), scatter_dimension=0, tiled=True
-        ),
-        lax.psum_scatter(
-            up_weight_grad.reshape(-1), ("batch", "seq"), scatter_dimension=0, tiled=True
-        ),
-        lax.psum_scatter(
-            down_weight_grad.reshape(-1), ("batch", "seq"), scatter_dimension=0, tiled=True
-        ),
-        lax.psum_scatter(attn_pack, ("batch", "seq"), scatter_dimension=0, tiled=True),
-        lax.psum_scatter(ffn_pack, ("batch", "seq"), scatter_dimension=0, tiled=True),
-    )
-    gathered = (
-        lax.all_gather(share_tuple[0], ("batch", "seq"), axis=0, tiled=True),
-        lax.all_gather(share_tuple[1], ("batch", "seq"), axis=0, tiled=True),
-        lax.all_gather(share_tuple[2], ("batch", "seq"), axis=0, tiled=True),
-        lax.all_gather(share_tuple[3], ("batch", "seq"), axis=0, tiled=True),
-        lax.all_gather(share_tuple[4], ("batch", "seq"), axis=0, tiled=True),
-        lax.all_gather(share_tuple[5], ("batch", "seq"), axis=0, tiled=True),
-    )
-    attn_small = unpack_vectors(
-        gathered[4],
+        ]
+    )
+    many, gathered, vector = grad_reduce(
+        down_weight_grad.astype(jnp.bfloat16),
+        up_weight_grad.astype(jnp.bfloat16),
+        out_weight_grad.astype(jnp.bfloat16),
+        qkv_grad.astype(jnp.bfloat16),
+        vector,
+        batch_size,
+        seq_size,
+    )
+    small = unpack_vectors(
+        vector.reshape(-1),
         [
+            ff_width,
+            model_width,
+            model_width,
+            model_width,
             model_width,
             model_width,
             head_count * tap_count,
@@ -376,26 +759,24 @@
             head_count,
         ],
     )
-    ffn_small = unpack_vectors(gathered[5], [ff_width, model_width, model_width, model_width])
-    condition = attn_small[6] / (device_total * seq_count)
     return (
         layer_out,
         input_grad,
-        gathered[0].reshape(model_width, 3 * model_width),
-        attn_small[0],
-        attn_small[1],
-        attn_small[2].reshape(head_count, tap_count),
-        gathered[1].reshape(model_width, model_width),
-        attn_small[3],
-        attn_small[4],
-        attn_small[5],
-        gathered[2].reshape(model_width, ff_width),
-        ffn_small[0],
-        gathered[3].reshape(ff_width, model_width),
-        ffn_small[1],
-        ffn_small[2],
-        ffn_small[3],
-        condition,
+        widen(gathered, many, 9, qkv_grad.shape),
+        small[4],
+        small[5],
+        small[6].reshape(head_count, tap_count),
+        widen(gathered, many, 8, out_weight_grad.shape),
+        small[7],
+        small[8],
+        small[9],
+        widen(gathered, many, 4, up_weight_grad.shape),
+        small[0],
+        widen(gathered, many, 0, down_weight_grad.shape),
+        small[1],
+        small[2],
+        small[3],
+        small[10] / (device_total * seq_count),
     )
 
 

time: 1290 us -> 757 us (0.59)
  waiting for transfers between devices: 580 us -> 54.1 us
  Pallas kernels: 0 us -> 159 us
  blocking collectives: 116 us -> 31.8 us
  local copies, waits for them, and re-layouts: 241 us -> 163 us
    unnamed x10 -> x4, waiting for transfers between devices: 432 us -> 0.07 us
    pallas_call x0 -> x5, Pallas kernels: none -> 159 us  [the longest x1 135 us: grad_reduce(): pl.pallas_call(partial(grad_kernel, batch_size, seq_size, plan, rows), ou...]
    unnamed x2 -> x0, blocking collectives: 83.8 us -> none
    all_gather x4 -> x0, waiting for transfers between devices: 68.1 us -> none  [the longest x1 68.1 us: body(): lax.all_gather(share_tuple[2], ('batch', 'seq'), axis=0, tiled=True)]
    reshape x8 -> x2, local copies, waits for them, and re-layouts: 56.7 us -> 2.08 us  [the longest x1 1.4 us: pack_vectors(): return jnp.pad(flat_vec, (0, -flat_vec.shape[0] % 1024)).reshape(-1, 128)]
    unnamed x347 -> x304, local copies, waits for them, and re-layouts: 74.5 us -> 54.2 us
    psum x1, waiting for transfers between devices: 15.9 us -> 0.01 us  [body(): grad_mixed = lax.psum(grad_mix_part, 'seq')]
  transfers between devices with their start and end apart: 13 -> 8, of which waited for: 6 -> 3; matrix products, arithmetic and copies ran while one was open for 31% -> 36% of each run, Pallas kernels for 0% -> 0%
where the time goes in v1:
time: 757 us; the launch traced here: 747 us
  matrix products  211 us (28%)
  local copies, waits for them, and re-layouts  163 us (22%)
  Pallas kernels  159 us (21%)
  other arithmetic  99.3 us (13%)
  waiting for transfers between devices  54.1 us (7%)
  blocking collectives  31.8 us (4%)
  between operations  16.1 us (2%)
  starting transfers between devices  12.3 us (2%)
    pallas_call x1, Pallas kernels, grad_reduce(): pl.pallas_call(partial(grad_kernel, batch_size, seq_size, plan, rows), ou...  135 us
    unnamed x304, local copies, waits for them, and re-layouts  54.2 us
    dot_general x36, matrix products, pseudo_inverse(): jnp.matmul(product, inner_term, precision=precise)  46.1 us
    another operation x34, local copies, waits for them, and re-layouts, body(): jnp.stack([jnp.sum(grad_branch_wide * padded_values[:, tap_index:tap_inde...  45.4 us
    psum x2, waiting for transfers between devices, landmark_total(): whole_sum = lax.psum(partial_sum, 'seq')  29.6 us
    dot_general x18, matrix products, pseudo_inverse(): product = jnp.matmul(kernel, approx, precision=precise)  29.3 us
    another operation x1, other arithmetic  26.2 us
    psum x1, waiting for transfers between devices, body(): acc_sum, exp_total = lax.psum((acc_part, jnp.sum(expo_val, axis=-1)), 'seq')  24.4 us
  transfers between devices with their start and end apart: 8, of which 3 were waited for; matrix products, arithmetic and copies ran while one was open for 36% of the time, Pallas kernels for 0%

profile of v1, /device:TPU:0, one launch (start us, length us, event | category | flops | bytes accessed | tf_op | source)
XLA Modules:
  0.0 746.6 jit_solution(4963748482354009106)
XLA Ops:
  10.5 3.1 convolution_add_fusion
  18.9 5.5 collective-permute-start
  45.4 24.8 %all-reduce.6.cloned.1.call-done = f32[2,2,64,768]{3,2,0,1:T(8,128)} async-done(((f32[2,2,64,768]{3,2,0,1:T(8,128)}), f32[2,2,64,768]{3,2,0,1:T(8,128)}) %all-reduce.6.cloned.1.call-update) | async-done | bytes 786448 | tf_op jit(solution)/shard_map/psum | solution.py:468
  114.2 16.3 %pmax.7 = f32[2,12,64]{2,1,0:T(8,128)} all-reduce(f32[2,12,64]{2,1,0:T(8,128)} %get-tuple-element.130), channel_id=1, replica_groups=mesh['batch'=8,'seq'=4] {'seq'}, use_global_device_ids=true, to_apply=%region_5.6 | all-reduce | flops 1536 | bytes 12288 | tf_op jit(solution)/shard_map/pmax | solution.py:558
  138.7 15.5 %psum.37 = f32[2,12,64]{2,1,0:T(8,128)} all-reduce(f32[2,12,64]{2,1,0:T(8,128)} %fusion.128), channel_id=1, replica_groups=mesh['batch'=8,'seq'=4] {'seq'}, use_global_device_ids=true, to_apply=%region_8.9 | all-reduce | flops 1536 | bytes 12288 | tf_op jit(solution)/shard_map/psum | solution.py:562
  154.2 4.0 fusion.259
  158.1 24.4 %all-reduce.8.cloned.1.call-done = f32[2,12,64,64]{3,2,1,0:T(8,128)} async-done(((f32[2,12,64,64]{3,2,1,0:T(8,128)}), f32[2,12,64,64]{3,2,1,0:T(8,128)}) %all-reduce.8.cloned.1.call-update) | async-done | bytes 393232 | tf_op jit(solution)/shard_map/psum | solution.py:562
  182.5 3.1 convolution_convert_fusion.4
  185.7 3.8 fusion.211
  192.5 24.4 %fusion.48 = bf16[2,256,768]{2,1,0:T(8,128)(2,1)S(1)} fusion(f32[2,256,768]{2,1,0:T(8,128)} %copy.215, bf16[2,256,768]{2,1,0:T(8,128)(2,1)} %get-tuple-element.101, bf16[2,16,768]{2,1,0:T(8,128)(2,1)} %collective-permute-done.1, bf16[2,16,768]{2,1,0:T(8,128)(2,1)} %collective-permute-done, f32[768]{0:T(1024)} %get-tuple-element.63, ...), kind=kLoop, calls=%fused_computation.193 | loop fusion | flops 77070336 | bytes 3345408 | tf_op jit(solution)/shard_map/convert_element_type | solution.py:579
  218.7 19.9 %multiply_convert_fusion = (bf16[512,3072]{1,0:T(8,128)(2,1)S(1)}, f32[512,3072]{1,0:T(8,128)}, f32[512,3072]{1,0:T(8,128)}) fusion(f32[3072]{0:T(1024)S(1)} %copy-done.122, bf16[768,3072]{1,0:T(8,128)(2,1)} %param.27, f32[512,768]{1,0:T(8,128)S(1)} %get-tuple-element.135, f32[768]{0:T(1024)S(1)} %copy-done.125, f32[768]{0:T(1024)S(1)} %copy-done.109, ...), kind=kOutput, calls=%fused_computation.41 | convolution fusion | flops 2521694208 | bytes 22042624 | tf_op jit(solution)/shard_map/dot_general | solution.py:590
  245.9 9.8 %convert_reduce_fusion = (f32[3072]{0:T(1024)}, bf16[512,3072]{1,0:T(8,128)(2,1)}) fusion(f32[512,3072]{1,0:T(8,128)} %get-tuple-element.100, bf16[3072,768]{1,0:T(8,128)(2,1)S(1)} %bitcast.339, f32[512,768]{1,0:T(8,128)S(1)} %get-tuple-element.98, f32[512,3072]{1,0:T(8,128)} %get-tuple-element.136, f32[3072]{0:T(1024)S(1)} %copy-done.122), kind=kOutput, calls=%fused_computation.39 | convolution fusion | flops 2443047936 | bytes 22044672 | tf_op jit(solution)/shard_map/nd,fd->nf/dot_general | solution.py:612
  255.8 5.6 multiply_reduce_fusion
  262.6 5.8 fusion.82
  273.7 3.7 fusion.208
  283.7 4.8 convolution_convert_fusion.refs_1_
  288.5 4.3 convolution_convert_fusion.1.refs_0_
  304.8 5.2 fusion.81
  320.7 6.0 fusion.98
  328.1 6.6 fusion.99
  408.7 4.0 collective-permute-start.2
  414.1 3.5 convolution_convert_fusion.2.refs_2_
  498.1 5.3 multiply_reduce_fusion.7
  508.7 26.2 %multiply_convert_fusion.1 = bf16[2,256,768]{2,1,0:T(8,128)(2,1)} fusion(f32[2,256,768]{2,1,0:T(8,128)} %copy.252, bf16[2,256,768]{2,1,0:T(8,128)(2,1)} %bitcast.302, bf16[2,16,768]{2,1,0:T(8,128)(2,1)} %collective-permute-done.3, bf16[2,16,768]{2,1,0:T(8,128)(2,1)} %collective-permute-done.2, f32[768]{0:T(1024)} %get-tuple-element.63, ...), kind=kLoop, calls=%fused_computation.266 | loop fusion | flops 77463552 | bytes 3347456 | tf_op jit(solution)/shard_map/convert.7
  548.2 3.1 copy.250
  551.3 4.7 all-reduce.12.cloned.1.call-done
  561.0 3.9 fusion.8.refs_3_
  568.8 135.4 %grad_reduce.1 = (bf16[6,2,1536,384]{3,2,1,0:T(8,128)(2,1)}, f32[80,128]{1,0:T(8,128)}) custom-call(bf16[3072,768]{1,0:T(8,128)(2,1)} %convolution_convert_fusion.1.refs_0_, bf16[768,3072]{1,0:T(8,128)(2,1)} %convolution_convert_fusion.refs_1_, bf16[768,768]{1,0:T(8,128)(2,1)} %convolution_convert_fusion.2.refs_2_, bf16[768,2304]{1,0:T(8,128)(2,1)} %fusion.8.refs_3_, ...), custom_call_target="tpu_custom_call" | custom-call | tf_op jit(solution)/shard_map/grad_reduce/pallas_call | solution.py:351
  704.2 7.7 %widen.6 = f32[768,3072]{1,0:T(8,128)} custom-call(bf16[6,2,1536,384]{3,2,1,0:T(8,128)(2,1)} %get-tuple-element.19.in_ref), custom_call_target="tpu_custom_call" | custom-call | tf_op jit(solution)/shard_map/widen/pallas_call | solution.py:387
  711.8 7.6 %widen.7 = f32[3072,768]{1,0:T(8,128)} custom-call(bf16[6,2,1536,384]{3,2,1,0:T(8,128)(2,1)} %get-tuple-element.19.in_ref), custom_call_target="tpu_custom_call" | custom-call | tf_op jit(solution)/shard_map/widen/pallas_call | solution.py:387
  719.5 6.0 widen.4
  734.1 5.0 add_convert_fusion.1
  (520 shorter events, 321.6 us)
Async XLA Ops:
  7.2 63.0 %all-reduce.6.cloned.1.call-start = ((), (), s32[]{:S(2)}) async-start(), calls=%async_computation | async-start | bytes 1572864 | tf_op jit(solution)/shard_map/psum | solution.py:468
  9.1 7.0 copy-start.90
  9.1 7.0 copy-start.92
  9.1 61.1 %copy-start.103 = (f32[2,64]{1,0:T(2,128)}, f32[2,64]{1,0:T(2,128)S(1)}, u32[]{:S(2)}) copy-start(f32[2,64]{1,0:T(2,128)S(1)} %get-tuple-element.125) | copy-start | bytes 1540
  9.1 7.0 copy-start.94
  16.5 9.2 %copy-start.88 = (f32[768]{0:T(1024)S(1)}, f32[768]{0:T(1024)}, u32[]{:S(2)}) copy-start(f32[768]{0:T(1024)} %param.31) | copy-start | bytes 9220
  17.4 165.1 %all-reduce.8.cloned.1.call-start = ((), (), s32[]{:S(2)}) async-start(), calls=%async_computation.1 | async-start | bytes 1572864 | tf_op jit(solution)/shard_map/psum | solution.py:562
  18.9 173.5 %collective-permute-start = (bf16[2,16,768]{2,1,0:T(8,128)(2,1)}, bf16[2,16,768]{2,1,0:T(8,128)(2,1)}, u32[]{:S(2)}, u32[]{:S(2)}) collective-permute-start(bf16[2,16,768]{2,1,0:T(8,128)(2,1)} %get-tuple-element.107), channel_id=1, source_target_pairs={{0,1},{1,2},{2,3},{4,5},{5,6},{6,7},{8,9},{9,10},{10,11},{12,13},{... | collective-permute-start | bytes 147464 | tf_op jit(solution)/shard_map/ppermute | solution.py:415
  24.4 168.1 %collective-permute-start.1 = (bf16[2,16,768]{2,1,0:T(8,128)(2,1)}, bf16[2,16,768]{2,1,0:T(8,128)(2,1)}, u32[]{:S(2)}, u32[]{:S(2)}) collective-permute-start(bf16[2,16,768]{2,1,0:T(8,128)(2,1)} %get-tuple-element.108), channel_id=1, source_target_pairs={{1,0},{2,1},{3,2},{5,4},{6,5},{7,6},{9,8},{10,9},{11,10},{13,12},{... | collective-permute-start | bytes 147464 | tf_op jit(solution)/shard_map/ppermute | solution.py:417
  78.8 26.3 %copy-start.1 = (f32[2,12,64,64]{2,3,1,0:T(8,128)}, f32[2,12,64,64]{2,3,1,0:T(8,128)S(1)}, u32[]{:S(2)}) copy-start(f32[2,12,64,64]{2,3,1,0:T(8,128)S(1)} %get-tuple-element.129) | copy-start | bytes 1179652
  133.5 284.1 %all-reduce.10.cloned.1.call-start = ((), (), s32[]{:S(2)}) async-start(), calls=%async_computation.2 | async-start | bytes 1572864 | tf_op jit(solution)/shard_map/psum | solution.py:641
  192.5 24.4 %copy-start.117 = (bf16[768,768]{1,0:T(8,128)(2,1)S(1)}, bf16[768,768]{1,0:T(8,128)(2,1)}, u32[]{:S(2)}) copy-start(bf16[768,768]{1,0:T(8,128)(2,1)} %param.23) | copy-start | bytes 3538948
  192.5 24.4 %copy-start.118 = (bf16[2,256,768]{2,1,0:T(8,128)(2,1)S(1)}, bf16[2,256,768]{2,1,0:T(8,128)(2,1)}, u32[]{:S(2)}) copy-start(bf16[2,256,768]{2,1,0:T(8,128)(2,1)} %param.17) | copy-start | bytes 2359300
  192.5 24.4 %copy-start.123 = (f32[768]{0:T(1024)S(1)}, f32[768]{0:T(1024)}, u32[]{:S(2)}) copy-start(f32[768]{0:T(1024)} %param.24) | copy-start | bytes 9220
  192.5 46.0 %slice-start = ((s8[4718592]{0:T(1024)(128)(4,1)}), s8[4194304]{0:T(1024)(128)(4,1)S(1)}, s32[]{:S(2)}) async-start(s8[4718592]{0:T(1024)(128)(4,1)} %bitcast.338), calls=%async_computation.4 | async-start | bytes 8388608
  217.8 43.6 %copy-start.60 = (f32[512,768]{1,0:T(8,128)}, f32[512,768]{1,0:T(8,128)S(1)}, u32[]{:S(2)}) copy-start(f32[512,768]{1,0:T(8,128)S(1)} %get-tuple-element.135) | copy-start | bytes 4718596
  217.9 43.5 %copy-start.96 = (f32[512]{0:T(512)}, f32[512]{0:T(512)S(1)}, u32[]{:S(2)}) copy-start(f32[512]{0:T(512)S(1)} %broadcast_multiply_fusion.4) | copy-start | bytes 6148
  218.7 42.8 %copy-start.106 = (f32[512]{0:T(512)}, f32[512]{0:T(512)S(1)}, u32[]{:S(2)}) copy-start(f32[512]{0:T(512)S(1)} %add_rsqrt_fusion.1) | copy-start | bytes 6148
  218.7 19.9 %slice-start.1 = ((s8[4718592]{0:T(1024)(128)(4,1)}), s8[524288]{0:T(1024)(128)(4,1)S(1)}, s32[]{:S(2)}) async-start(s8[4718592]{0:T(1024)(128)(4,1)} %bitcast.338), calls=%async_computation.5 | async-start | bytes 1048576
  218.7 19.9 %copy-start.124 = (f32[768]{0:T(1024)S(1)}, f32[768]{0:T(1024)}, u32[]{:S(2)}) copy-start(f32[768]{0:T(1024)} %param.30) | copy-start | bytes 9220
  243.8 12.0 %slice-start.2 = ((s8[4718592]{0:T(1024)(128)(4,1)}), s8[4194304]{0:T(1024)(128)(4,1)S(1)}, s32[]{:S(2)}) async-start(s8[4718592]{0:T(1024)(128)(4,1)} %bitcast.340), calls=%async_computation.6 | async-start | bytes 8388608
  245.9 9.9 %copy-start.78 = (f32[512,768]{1,0:T(8,128)}, f32[512,768]{1,0:T(8,128)S(1)}, u32[]{:S(2)}) copy-start(f32[512,768]{1,0:T(8,128)S(1)} %get-tuple-element.98) | copy-start | bytes 4718596
  245.9 9.9 %slice-start.3 = ((s8[4718592]{0:T(1024)(128)(4,1)}), s8[524288]{0:T(1024)(128)(4,1)S(1)}, s32[]{:S(2)}) async-start(s8[4718592]{0:T(1024)(128)(4,1)} %bitcast.340), calls=%async_computation.7 | async-start | bytes 1048576
  356.1 199.9 %all-reduce.12.cloned.1.call-start = ((), (), s32[]{:S(2)}) async-start(), calls=%async_computation.3 | async-start | bytes 1572864 | tf_op jit(solution)/shard_map/psum | solution.py:468
  408.7 100.0 %collective-permute-start.2 = (bf16[2,16,768]{2,1,0:T(8,128)(2,1)}, bf16[2,16,768]{2,1,0:T(8,128)(2,1)}, u32[]{:S(2)}, u32[]{:S(2)}) collective-permute-start(bf16[2,16,768]{2,1,0:T(8,128)(2,1)} %get-tuple-element.105), channel_id=1, source_target_pairs={{0,1},{1,2},{2,3},{4,5},{5,6},{6,7},{8,9},{9,10},{10,11},{12,13},{... | collective-permute-start | bytes 147464 | tf_op jit(solution)/shard_map/ppermute | solution.py:415
  412.6 96.1 %collective-permute-start.3 = (bf16[2,16,768]{2,1,0:T(8,128)(2,1)}, bf16[2,16,768]{2,1,0:T(8,128)(2,1)}, u32[]{:S(2)}, u32[]{:S(2)}) collective-permute-start(bf16[2,16,768]{2,1,0:T(8,128)(2,1)} %get-tuple-element.106), channel_id=1, source_target_pairs={{1,0},{2,1},{3,2},{5,4},{6,5},{7,6},{9,8},{10,9},{11,10},{13,12},{... | collective-permute-start | bytes 147464 | tf_op jit(solution)/shard_map/ppermute | solution.py:417
  508.7 26.2 %copy-start.3 = (f32[2,12,64,64]{2,3,1,0:T(8,128)S(1)}, f32[2,12,64,64]{2,3,1,0:T(8,128)}, u32[]{:S(2)}) copy-start(f32[2,12,64,64]{2,3,1,0:T(8,128)} %copy-done.1) | copy-start | bytes 1179652
  508.7 26.2 %copy-start.65 = (bf16[2,1,64,768]{2,3,0,1:T(8,128)(2,1)S(1)}, bf16[2,1,64,768]{2,3,0,1:T(8,128)(2,1)}, u32[]{:S(2)}) copy-start(bf16[2,1,64,768]{2,3,0,1:T(8,128)(2,1)} %copy.291) | copy-start | bytes 589828
  508.7 26.2 %copy-start.102 = (f32[2,12,64]{2,1,0:T(8,128)S(1)}, f32[2,12,64]{2,1,0:T(8,128)}, u32[]{:S(2)}) copy-start(f32[2,12,64]{2,1,0:T(8,128)} %neg.98) | copy-start | bytes 18436
  508.7 26.3 %copy-start.127 = (f32[2,12,64,64]{2,3,1,0:T(8,128)S(1)}, f32[2,12,64,64]{2,3,1,0:T(8,128)}, u32[]{:S(2)}) copy-start(f32[2,12,64,64]{2,3,1,0:T(8,128)} %get-tuple-element.149) | copy-start | bytes 1179652
  548.2 7.8 %copy-start.104 = (f32[2,64]{1,0:T(2,128)S(1)}, f32[2,64]{1,0:T(2,128)}, u32[]{:S(2)}) copy-start(f32[2,64]{1,0:T(2,128)} %copy-done.103) | copy-start | bytes 1540
  551.3 6.4 copy-start.95
  (111 other events, 247.7 us)
Sparse Core Ops, SparseCore 0:
  17.6 52.5 all-reduce.5
  133.6 48.9 all-reduce.7
  356.2 48.7 all-reduce.9
  505.8 50.2 all-reduce.11
